TPU v7x, 256 devices: a whole 4x4x8 slice. The times are simulated.
256 devices in a mesh: dp: 4 (over y), row: 8 (over x, core), col: 8 (over z).
Axes of the slice: x: 4, y: 4, z: 8, core: 2. Of those that a mesh axis runs over, the one named last changes fastest.
Arguments:
- grad_parts: bfloat16 [4, 4096, 14336], P('dp', 'row', 'col'), may hold values from -3 to 3
- momentum: bfloat16 [4096, 14336], P(('row', 'dp'), 'col'), may hold values from -96 to 96
- right_prev: bfloat16 [14336, 128], P('col'), may hold values from -0.046875 to 0.046875
Outputs:
- momentum_next: bfloat16 [4096, 14336], P(('row', 'dp'), 'col')
- right_next: bfloat16 [14336, 128], P('col')
- update: bfloat16 [4096, 14336], P(('row', 'dp'), 'col')
All inputs are finite; a program needn't handle non-finite values.
Results may differ from a plain program's by a relative error of at most 0.024.
Values may be sent and summed in bfloat16 or wider, within the bound.
A program may use at most 64 MiB of HBM per device.

v0:
```python
import functools
import math

import jax
import jax.numpy as jnp
from jax import lax
from jax.experimental import pallas as pl
from jax.experimental.pallas import tpu as pltpu
from jax.sharding import PartitionSpec as P

f32 = jnp.float32
bf16 = jnp.bfloat16
HIGHEST = lax.Precision.HIGHEST
MESH = pl.DeviceIdType.MESH
RANK = 128
ROWS_DEV = 128
PANEL = 8
VMEM_BYTES = 63 * 1024 * 1024
CUTS = [(0, 384), (384, 256), (640, 256)]
LAST = [(0, 384), (384, 256), (640, 256)]
EARLY = 2


def nt(a, b, precision=None):
    return lax.dot_general(a, b, (((1,), (1,)), ((), ())), precision=precision, preferred_element_type=f32)


def nn(a, b, precision=None):
    return lax.dot_general(a, b, (((1,), (0,)), ((), ())), precision=precision, preferred_element_type=f32)


def halves(x):
    high = x.astype(bf16)
    return high, (x - high.astype(f32)).astype(bf16)


def nn3(a, b):
    a_high, a_low = halves(a)
    b_high, b_low = halves(b)
    return nn(a_high, b_high) + (nn(a_high, b_low) + nn(a_low, b_high))


def inverse_cholesky(a, ahead=2):
    n, count = RANK, RANK // PANEL
    rows = [a[PANEL * i : PANEL * (i + 1), :] for i in range(count)]
    row = lax.broadcasted_iota(jnp.int32, (PANEL, n), 0)
    lane = lax.broadcasted_iota(jnp.int32, (PANEL, n), 1)
    inv = [(lane == row + PANEL * i).astype(f32) for i in range(count)]
    out = []
    for b in range(count):
        end = min(count, b + 1 + ahead)
        cols = [
            [jnp.broadcast_to(rows[i][:, PANEL * b + k : PANEL * b + k + 1], (PANEL, n)) for k in range(PANEL)]
            for i in range(b, end)
        ]
        recips = []
        for j in range(PANEL):
            recip = 1.0 / jnp.broadcast_to(cols[0][j][j : j + 1, :], (PANEL, n))
            recips.append(recip)
            pivots = [jnp.broadcast_to(cols[0][k][j : j + 1, :], (PANEL, n)) for k in range(j + 1, PANEL)]
            row_a = jnp.broadcast_to(rows[b][j : j + 1, :], (PANEL, n))
            row_w = jnp.broadcast_to(inv[b][j : j + 1, :], (PANEL, n))
            for i in range(b, end):
                m = cols[i - b][j] * recip
                if i == b:
                    m = jnp.where(row > j, m, 0.0)
                for k in range(j + 1, PANEL):
                    cols[i - b][k] = cols[i - b][k] - m * pivots[k - j - 1]
                rows[i] = rows[i] - m * row_a
                inv[i] = inv[i] - m * row_w
        scale = recips[0]
        for j in range(1, PANEL):
            scale = jnp.where(row == j, recips[j], scale)
        out.append(inv[b] * jnp.sqrt(scale))
        if end < count:
            left = jnp.transpose(rows[b] * scale)[PANEL * end :, :]
            update = nn(left, jnp.concatenate([rows[b], inv[b]], 1), HIGHEST)
            for i in range(end, count):
                part = update[PANEL * (i - end) : PANEL * (i - end + 1), :]
                rows[i] = rows[i] - part[:, :n]
                inv[i] = inv[i] - part[:, n:]
    return jnp.concatenate(out, 0)


def column(row):
    return jnp.transpose(jnp.broadcast_to(row, (RANK, RANK)))


def kernel(
    ny, nx, nz, cols,
    grads, mom_hbm, right_hbm,
    mom_out, right_out, basis_out,
    g_all, g_relay, g_direct, g_mixed, g_summed, mom, right0, buf2,
    p1_part, p1_recv, zbuf, z_part, z_recv,
    chip_buf, chip_power, m_own, m_slots, m_full, m_other,
    g_core, g_slots, g_full,
    n_mine, n1_recv, n2_recv, back_own, back_other, mom_next, right_next, basis_next,
    local_sem, send, recv,
):
    half = cols // 2
    chips = ny * nx
    zr = RANK // nz
    cr = RANK // chips
    y = lax.axis_index("dp")
    r = lax.axis_index("row")
    z = lax.axis_index("col")
    x = r // 2
    c = lax.rem(r, 2)

    def dev(dy=0, dx=0, dc=0, dz=0):
        return {
            "dp": lax.rem(y + dy, ny),
            "row": lax.rem(x + dx, nx) * 2 + lax.rem(c + dc, 2),
            "col": lax.rem(z + dz, nz),
        }

    def hops(d, n):
        return min(d, n - d)

    yz = [(dy, dz) for dz in range(nz) for dy in range(ny) if dy or dz]
    yz.sort(key=lambda d: -hops(d[0], ny) - hops(d[1], nz))
    plane = [(dy, dx) for dy in range(ny) for dx in range(nx) if dy or dx]
    plane.sort(key=lambda d: -hops(d[0], ny) - hops(d[1], nx))
    along_z = sorted(range(1, nz), key=lambda d: -hops(d, nz))
    zc = [(dz, dc) for dz in range(nz) for dc in range(2) if dz or dc]

    met = []
    for dy, dz in yz:
        met.append((dy, 0, 0, dz))
    for dy, dx in plane:
        if (dy, dx, 0, 0) not in met:
            met.append((dy, dx, 0, 0))
    for dz, dc in zc:
        if (0, 0, dc, dz) not in met:
            met.append((0, 0, dc, dz))
    loads = []
    for i, (src, dst) in enumerate([(right_hbm, right0), (grads.at[0], g_all), (mom_hbm, mom)]):
        copy = pltpu.make_async_copy(src, dst, local_sem.at[i])
        copy.start()
        loads.append(copy)
    barrier = pltpu.get_barrier_semaphore()
    for offsets in met:
        pl.semaphore_signal(barrier, inc=1, device_id=dev(*offsets), device_id_type=MESH)

    sent = []

    slots = {}

    def slot_of(name):
        return slots.setdefault(name, len(slots))

    def put(src, dst, name, target):
        slot = slot_of(name)
        pltpu.make_async_remote_copy(
            src_ref=src, dst_ref=dst, send_sem=send.at[slot], recv_sem=recv.at[slot],
            device_id=target, device_id_type=MESH,
        ).start()

    def landed(ref, name):
        slot = slot_of(name)
        copy = pltpu.make_async_remote_copy(
            src_ref=ref, dst_ref=ref, send_sem=send.at[slot], recv_sem=recv.at[slot],
            device_id=dev(), device_id_type=MESH,
        )
        copy.wait_recv()
        sent.append(copy)

    cuts = CUTS
    last = LAST
    hr = ROWS_DEV // 2

    def columns(k):
        first, size = cuts[k]
        return [pl.ds(first, size), pl.ds(half + first, size)]

    def part_rows(owner, start):
        return pl.ds(pl.multiple_of(owner * ROWS_DEV + start, hr), hr)

    after, opposite, before = lax.rem(y + 1, ny), lax.rem(y + 2, ny), lax.rem(y + 3, ny)

    def put_relay(k):
        for where in columns(k):
            put(g_all.at[part_rows(opposite, 0), where], g_relay.at[0, :, where], f"relay {k}", dev(1))
            put(g_all.at[part_rows(opposite, hr), where], g_relay.at[1, :, where], f"relay {k}", dev(3))

    def put_direct(k):
        for where in columns(k):
            put(g_all.at[part_rows(after, hr), where], g_direct.at[1, :, where], f"direct {k}", dev(1))
            put(g_all.at[part_rows(before, 0), where], g_direct.at[0, :, where], f"direct {k}", dev(3))

    def both_columns(ref, k):
        return ref.at[:, :, pl.ds(0, 2 * cuts[k][1])]

    def put_mixed(k):
        landed(both_columns(g_relay, k), f"relay {k}")
        for where in columns(k):
            for side, (owner, start, dy) in enumerate([(after, 0, 1), (before, hr, 3)]):
                own = g_all[part_rows(owner, start), where].astype(f32)
                g_mixed[side, :, where] = (own + g_relay[side, :, where].astype(f32)).astype(bf16)
                put(g_mixed.at[side, :, where], g_summed.at[side, :, where], f"summed {k}", dev(dy))

    def make_buffer(k):
        landed(both_columns(g_direct, k), f"direct {k}")
        landed(both_columns(g_summed, k), f"summed {k}")
        for where in columns(k):
            for side in range(2):
                rows = pl.ds(side * hr, hr)
                total = g_all[part_rows(y, side * hr), where].astype(f32)
                total = total + g_direct[side, :, where].astype(f32) + g_summed[side, :, where].astype(f32)
                buffer = (mom[rows, where].astype(f32) + total).astype(bf16)
                buf2[rows, where] = buffer
        first, size = cuts[k]
        ours = pl.ds(pl.multiple_of(c * half + first, 128), size)
        theirs = pl.ds(pl.multiple_of((1 - c) * half + first, 128), size)
        chip_buf[c, :, pl.ds(first, size)] = buf2[:, ours]
        put(buf2.at[:, theirs], chip_buf.at[c, :, pl.ds(first, size)], f"buffer {k}", dev(0, 0, 1))

    loads[0].wait()
    right_t = jnp.transpose(right0[...])
    loads[1].wait()
    for i in range(ny):
        if i == EARLY:
            pl.semaphore_wait(barrier, len(met))
            put_relay(0)
        p1_part[i] = nt(right_t, g_all[pl.ds(i * ROWS_DEV, ROWS_DEV), :])
    loads[2].wait()
    p1_part[y] = p1_part[y] + nt(right_t, mom[...])
    for i, (dy, dz) in enumerate(yz):
        there_y, there_z = lax.rem(y + dy, ny), lax.rem(z + dz, nz)
        put(
            p1_part.at[there_y, pl.ds(pl.multiple_of(there_z * zr, zr), zr), :], p1_recv.at[i],
            "power parts", dev(dy, 0, 0, dz),
        )
    put_relay(1)
    put_direct(0)
    put_relay(2)
    put_direct(1)
    put_mixed(0)
    put_direct(2)
    put_mixed(1)
    z_rows = pl.ds(pl.multiple_of(z * zr, zr), zr)

    def gather_z(step, slot):
        for dz in along_z:
            put(zbuf.at[step, z_rows, :], zbuf.at[step, z_rows, :], slot, dev(0, 0, 0, dz))

    landed(p1_recv, "power parts")
    total = p1_part[y, z_rows, :]
    for i in range(len(yz)):
        total = total + p1_recv[i]
    zbuf[0, z_rows, :] = total
    gather_z(0, "power 1")
    put_mixed(2)
    landed(z_recv, "power 1")

    mine = pl.ds(pl.multiple_of(c * half, 128), half)
    others = pl.ds(pl.multiple_of((1 - c) * half, 128), half)
    here = y * nx + x
    chip_rows = pl.ds(pl.multiple_of(here * cr, cr), cr)

    def to_plane(name, src, dst):
        for i, (dy, dx) in enumerate(plane):
            there = lax.rem(y + dy, ny) * nx + lax.rem(x + dx, nx)
            rows = pl.ds(pl.multiple_of(there * cr, cr), cr)
            put(src(rows), dst(i), name, dev(dy, dx))

    def reduce_plane(step, power):
        cuts = CUTS if step == 0 else LAST
        chip_power[step, c] = power
        put(chip_power.at[step, c], chip_power.at[step, c], f"power core {step}", dev(0, 0, 1))
        landed(chip_power.at[step, 0], f"power core {step}")
        power = jnp.concatenate([chip_power[step, 0], chip_power[step, 1]], 1)
        high, low = halves(power)

        def product(k):
            where = pl.ds(*cuts[k])
            rows = jnp.concatenate([chip_buf[0, :, where], chip_buf[1, :, where]], 0)
            m_own[step, :, where] = nn(high, rows) + nn(low, rows)

        def parts(k):
            where = pl.ds(*cuts[k])
            to_plane(
                f"back parts {step}{k}",
                lambda rows: m_own.at[step, rows, where], lambda i: m_slots.at[step, i, :, where],
            )

        def gram_parts():
            g_core[step] = nt(power, power, HIGHEST)
            to_plane(f"gram parts {step}", lambda rows: g_core.at[step, rows, :], lambda i: g_slots.at[step, i])

        for k in range(len(cuts)):
            if step == 0:
                make_buffer(k)
                if k == 0:
                    gram_parts()
                landed(chip_buf.at[0, :, pl.ds(*cuts[k])], f"buffer {k}")
            if step == 1 and k == 0:
                gram_parts()
            product(k)
            parts(k)
        landed(g_slots.at[step], f"gram parts {step}")
        total = g_core[step, chip_rows, :]
        for i in range(len(plane)):
            total = total + g_slots[step, i]
        g_full[step, chip_rows, :] = total
        for dy, dx in plane:
            put(g_full.at[step, chip_rows, :], g_full.at[step, chip_rows, :], f"gram {step}", dev(dy, dx))
        for k, (first, size) in enumerate(cuts):
            where = pl.ds(first, size)
            landed(m_slots.at[step, :, :, where], f"back parts {step}{k}")
            total = m_own[step, chip_rows, where]
            for i in range(len(plane)):
                total = total + m_slots[step, i, :, where]
            m_full[step, chip_rows, where] = total
            for dy, dx in plane:
                block = m_full.at[step, chip_rows, where]
                put(block, block, f"back {step}{k}", dev(dy, dx))

    def gram_done(step):
        landed(g_slots.at[step], f"gram {step}")
        return g_full[step]

    def back_done(step, k):
        landed(m_slots.at[step, :, :, pl.ds(*(cuts, last)[step][k])], f"back {step}{k}")

    reduce_plane(0, zbuf[0])
    next_part = jnp.zeros((2 * RANK, ROWS_DEV), f32)
    for k, (first, size) in enumerate(cuts):
        where = pl.ds(first, size)
        back_done(0, k)
        put(m_full.at[0, :, where], m_other.at[:, where], f"back other {k}", dev(0, 0, 1))
        both = jnp.concatenate(halves(m_full[0, :, where]), 0)
        next_part = next_part + nt(both, buf2[:, pl.ds(pl.multiple_of(c * half + first, 128), size)])
    for k, (first, size) in enumerate(cuts):
        where = pl.ds(first, size)
        landed(m_other.at[:, where], f"back other {k}")
        both = jnp.concatenate(halves(m_other[:, where]), 0)
        next_part = next_part + nt(both, buf2[:, pl.ds(pl.multiple_of((1 - c) * half + first, 128), size)])
    z_part[...] = next_part[:RANK] + next_part[RANK:]
    for dz in along_z:
        there = lax.rem(z + dz, nz)
        put(z_part.at[pl.ds(pl.multiple_of(there * zr, zr), zr), :], z_recv.at[dz - 1], "power 2 parts", dev(0, 0, 0, dz))
    w1 = inverse_cholesky(gram_done(0))
    landed(z_recv, "power 2 parts")
    total = z_part[z_rows, :]
    for i in range(nz - 1):
        total = total + z_recv[i]
    zbuf[1, z_rows, :] = total
    gather_z(1, "power 2")
    back_a = nn3(w1, m_full[0])
    back_b = nn3(w1, m_other[...])
    own_sum = jnp.sum(back_a * back_a, axis=1, keepdims=True) + jnp.sum(back_b * back_b, axis=1, keepdims=True)
    own_col = jnp.broadcast_to(own_sum, (RANK, RANK))
    own_row = jnp.transpose(own_col)
    n_mine[0] = own_row[0:8, :]
    for dz in along_z:
        put(n_mine.at[0], n1_recv.at[dz - 1], "norms 1", dev(0, 0, 0, dz))
    landed(z_recv, "power 2")

    power = nn(w1, zbuf[1], HIGHEST) * lax.rsqrt(own_col + 1e-6)
    reduce_plane(1, power)
    landed(n1_recv, "norms 1")
    norm = own_row[0:1, :]
    for i in range(nz - 1):
        norm = norm + n1_recv[i, 0:1, :]
    rest = jnp.sqrt((own_row[0:1, :] + 1e-6) / (norm + 1e-6))
    gram = gram_done(1) * column(rest) * rest
    w2 = inverse_cholesky(gram) * rest
    part = jnp.zeros((1, RANK), f32)
    for k, (first, size) in enumerate(last):
        where = pl.ds(first, size)
        back_done(1, k)
        back = jnp.transpose(nn3(w2, m_full[1, :, where]))
        part = part + jnp.sum(back * back, axis=0, keepdims=True)
        back_own[where, :] = back
    n_mine[1] = jnp.broadcast_to(part, (8, RANK))
    for i, (dz, dc) in enumerate(zc):
        put(n_mine.at[1], n2_recv.at[i], "norms 2", dev(0, 0, dc, dz))
    put(back_own, back_other, "last back", dev(0, 0, 1))
    basis = jnp.transpose(nn(w2, power, HIGHEST)).astype(bf16)
    mom_next[:, mine] = (
        buf2[:, mine].astype(f32) - 0.25 * nt(basis, back_own[...].astype(bf16))
    ).astype(bf16)
    basis_next[...] = basis
    landed(back_other, "last back")
    mom_next[:, others] = (
        buf2[:, others].astype(f32) - 0.25 * nt(basis, back_other[...].astype(bf16))
    ).astype(bf16)
    stores = [
        pltpu.make_async_copy(mom_next, mom_out, local_sem.at[3]),
        pltpu.make_async_copy(basis_next, basis_out, local_sem.at[4]),
        pltpu.make_async_copy(right_next, right_out, local_sem.at[5]),
    ]
    stores[0].start()
    stores[1].start()
    landed(n2_recv, "norms 2")
    norm = part
    for i in range(len(zc)):
        norm = norm + n2_recv[i, 0:1, :]
    scale = lax.rsqrt(norm + 1e-6)
    right_next[mine, :] = (back_own[...] * scale).astype(bf16)
    right_next[others, :] = (back_other[...] * scale).astype(bf16)
    stores[2].start()
    for copy in sent:
        copy.wait_send()
    for copy in stores:
        copy.wait()


def finish(factor, mom_in, right_in, basis_in, mom_out, right_out, upd_out, mom, right, basis, upd, sem):
    loads = [
        pltpu.make_async_copy(src, dst, sem.at[i])
        for i, (src, dst) in enumerate([(basis_in, basis), (right_in, right), (mom_in, mom)])
    ]
    for copy in loads:
        copy.start()
    stores = [pltpu.make_async_copy(right, right_out, sem.at[3]), pltpu.make_async_copy(mom, mom_out, sem.at[4])]
    loads[0].wait()
    loads[1].wait()
    stores[0].start()
    half = upd.shape[1] // 2
    for i in range(2):
        where = pl.ds(i * half, half)
        upd[:, where] = (factor * nt(basis[...], right[where, :])).astype(bf16)
        if i == 0:
            loads[2].wait()
            stores[1].start()
        stores.append(pltpu.make_async_copy(upd.at[:, where], upd_out.at[:, where], sem.at[5 + i]))
        stores[-1].start()
    for copy in stores:
        copy.wait()


def solution(mesh):
    ny, nx, nz = mesh.shape["dp"], mesh.shape["row"] // 2, mesh.shape["col"]

    def on_device(grad_parts, momentum, right_prev):
        cols = momentum.shape[1]
        half, chips = cols // 2, ny * nx
        zr, cr = RANK // nz, RANK // chips
        factor = math.sqrt(ny * nx * 2 * ROWS_DEV * cols * nz / RANK)
        vmem = pltpu.VMEM
        any_space = pl.BlockSpec(memory_space=pl.ANY)
        mom_shape = jax.ShapeDtypeStruct((ROWS_DEV, cols), bf16)
        right_shape = jax.ShapeDtypeStruct((cols, RANK), bf16)
        results = pl.pallas_call(
            functools.partial(kernel, ny, nx, nz, cols),
            out_shape=(mom_shape, right_shape, jax.ShapeDtypeStruct((ROWS_DEV, RANK), bf16)),
            in_specs=[any_space] * 3,
            out_specs=(any_space,) * 3,
            scratch_shapes=[
                vmem((ny * ROWS_DEV, cols), bf16),
                vmem((2, ROWS_DEV // 2, cols), bf16),
                vmem((2, ROWS_DEV // 2, cols), bf16),
                vmem((2, ROWS_DEV // 2, cols), bf16),
                vmem((2, ROWS_DEV // 2, cols), bf16),
                vmem((ROWS_DEV, cols), bf16),
                vmem((cols, RANK), bf16),
                vmem((ROWS_DEV, cols), bf16),
                vmem((ny, RANK, ROWS_DEV), f32),
                vmem((ny * nz - 1, zr, ROWS_DEV), f32),
                vmem((2, RANK, ROWS_DEV), f32),
                vmem((RANK, ROWS_DEV), f32),
                vmem((nz - 1, zr, ROWS_DEV), f32),
                vmem((2, ROWS_DEV, half), bf16),
                vmem((2, 2, RANK, ROWS_DEV), f32),
                vmem((2, RANK, half), f32),
                vmem((2, chips - 1, cr, half), f32),
                vmem((2, RANK, half), f32),
                vmem((RANK, half), f32),
                vmem((2, RANK, RANK), f32),
                vmem((2, chips - 1, cr, RANK), f32),
                vmem((2, RANK, RANK), f32),
                vmem((2, 8, RANK), f32),
                vmem((nz - 1, 8, RANK), f32),
                vmem((2 * nz - 1, 8, RANK), f32),
                vmem((half, RANK), f32),
                vmem((half, RANK), f32),
                vmem((ROWS_DEV, cols), bf16),
                vmem((cols, RANK), bf16),
                vmem((ROWS_DEV, RANK), bf16),
                pltpu.SemaphoreType.DMA((6,)),
                pltpu.SemaphoreType.DMA((48,)),
                pltpu.SemaphoreType.DMA((48,)),
            ],
            compiler_params=pltpu.CompilerParams(
                collective_id=0, has_side_effects=True, vmem_limit_bytes=VMEM_BYTES
            ),
            cost_estimate=pl.CostEstimate(flops=10**9, bytes_accessed=4 * 10**6, transcendentals=0),
        )(grad_parts, momentum, right_prev)
        return pl.pallas_call(
            functools.partial(finish, factor),
            out_shape=(mom_shape, right_shape, mom_shape),
            in_specs=[any_space] * 3,
            out_specs=(any_space,) * 3,
            scratch_shapes=[
                vmem((ROWS_DEV, cols), bf16),
                vmem((cols, RANK), bf16),
                vmem((ROWS_DEV, RANK), bf16),
                vmem((ROWS_DEV, cols), bf16),
                pltpu.SemaphoreType.DMA((7,)),
            ],
            compiler_params=pltpu.CompilerParams(vmem_limit_bytes=VMEM_BYTES),
            cost_estimate=pl.CostEstimate(flops=6 * 10**7, bytes_accessed=3 * 10**6, transcendentals=0),
        )(*results)

    return jax.shard_map(
        on_device,
        mesh=mesh,
        in_specs=(P("dp", "row", "col"), P(("row", "dp"), "col"), P("col", None)),
        out_specs=(P(("row", "dp"), "col"), P("col", None), P(("row", "dp"), "col")),
        check_vma=False,
    )
```

profile of v0, /device:TPU:1, one launch (start us, length us, event | category | flops | bytes accessed | tf_op | source)
XLA Modules:
  0.0 80.1 jit_solution(2547695033315726124)
XLA Ops:
  0.6 77.3 %shard_map.58 = (bf16[128,1792]{1,0:T(8,128)(2,1)}, bf16[1792,128]{1,0:T(8,128)(2,1)}, bf16[128,128]{1,0:T(8,128)(2,1)}) custom-call(bf16[1,512,1792]{2,1,0:T(8,128)(2,1)} %grads.1, bf16[128,1792]{1,0:T(8,128)(2,1)} %mom_hbm.1, bf16[1792,128]{1,0:T(8,128)(2,1)} %right_hbm.1), custom_call_target="tpu_custom_call" | custom-call | flops 1000000000 | bytes 4000000 | tf_op jit(solution)/shard_map/pallas_call | solution.py:446
  77.9 2.3 %shard_map.59 = (bf16[128,1792]{1,0:T(8,128)(2,1)}, bf16[1792,128]{1,0:T(8,128)(2,1)}, bf16[128,1792]{1,0:T(8,128)(2,1)}) custom-call(bf16[128,1792]{1,0:T(8,128)(2,1)} %get-tuple-element.6.mom_in, bf16[1792,128]{1,0:T(8,128)(2,1)} %get-tuple-element.7.right_in, bf16[128,128]{1,0:T(8,128)(2,1)} %get-tuple-element.8.basis_in), custom_call_target="tpu_custom_call" | custom-call | flops 60000000 | bytes 3000000 | tf_op jit(solution)/shard_map/pallas_call | solution.py:491
where the time goes:
time: 80.3 us; the launch traced here: 80.1 us
  Pallas kernels  79.5 us (99%)
    pallas_call x1, Pallas kernels, on_device(): pl.pallas_call(functools.partial(kernel, ny, nx, nz, cols), out_shape=(mo...  77.3 us
    pallas_call x1, Pallas kernels, on_device(): pl.pallas_call(functools.partial(finish, factor), out_shape=(mom_shape, r...  2.25 us

commit v1 on v0

--- a/solution.py
+++ b/solution.py
@@ -120,7 +120,7 @@
     yz = [(dy, dz) for dz in range(nz) for dy in range(ny) if dy or dz]
     yz.sort(key=lambda d: -hops(d[0], ny) - hops(d[1], nz))
     plane = [(dy, dx) for dy in range(ny) for dx in range(nx) if dy or dx]
-    plane.sort(key=lambda d: -hops(d[0], ny) - hops(d[1], nx))
+    plane.sort(key=lambda d: (-hops(d[0], ny), -hops(d[1], nx)))
     along_z = sorted(range(1, nz), key=lambda d: -hops(d, nz))
     zc = [(dz, dc) for dz in range(nz) for dc in range(2) if dz or dc]
 

time: 80.3 us -> 80.3 us (level)
  no operation moved by 1% of the time
where the time goes in v1:
time: 80.3 us; the launch traced here: 80.2 us
  Pallas kernels  79.6 us (99%)
    pallas_call x1, Pallas kernels, on_device(): pl.pallas_call(functools.partial(kernel, ny, nx, nz, cols), out_shape=(mo...  77.3 us
    pallas_call x1, Pallas kernels, on_device(): pl.pallas_call(functools.partial(finish, factor), out_shape=(mom_shape, r...  2.25 us

profile of v1, /device:TPU:1, one launch (start us, length us, event | category | flops | bytes accessed | tf_op | source)
XLA Modules:
  0.0 80.2 jit_solution(10588702732637660881)
XLA Ops:
  0.6 77.3 %shard_map.58 = (bf16[128,1792]{1,0:T(8,128)(2,1)}, bf16[1792,128]{1,0:T(8,128)(2,1)}, bf16[128,128]{1,0:T(8,128)(2,1)}) custom-call(bf16[1,512,1792]{2,1,0:T(8,128)(2,1)} %grads.1, bf16[128,1792]{1,0:T(8,128)(2,1)} %mom_hbm.1, bf16[1792,128]{1,0:T(8,128)(2,1)} %right_hbm.1), custom_call_target="tpu_custom_call" | custom-call | flops 1000000000 | bytes 4000000 | tf_op jit(solution)/shard_map/pallas_call | solution.py:446
  78.0 2.3 %shard_map.59 = (bf16[128,1792]{1,0:T(8,128)(2,1)}, bf16[1792,128]{1,0:T(8,128)(2,1)}, bf16[128,1792]{1,0:T(8,128)(2,1)}) custom-call(bf16[128,1792]{1,0:T(8,128)(2,1)} %get-tuple-element.6.mom_in, bf16[1792,128]{1,0:T(8,128)(2,1)} %get-tuple-element.7.right_in, bf16[128,128]{1,0:T(8,128)(2,1)} %get-tuple-element.8.basis_in), custom_call_target="tpu_custom_call" | custom-call | flops 60000000 | bytes 3000000 | tf_op jit(solution)/shard_map/pallas_call | solution.py:491
